TPU v7x, 32 devices: a whole 2x2x4 slice. The times are simulated.
32 devices in a mesh: dp: 2 (over x), context: 4 (over y, core), expert: 4 (over z).
Axes of the slice: x: 2, y: 2, z: 4, core: 2. Of those that a mesh axis runs over, the one named last changes fastest.
Arguments:
- tokens: bfloat16 [8, 1024, 768], P(('dp', 'expert'), 'context'), may hold values from -6 to 6
- norm1_gain: float32 [768], replicated, may hold values from 0.1 to 1.9
- w_qkv: bfloat16 [768, 2304], replicated, may hold values from -0.21875 to 0.21875
- w_out: bfloat16 [768, 768], replicated, may hold values from -1.75 to 1.75
- bias_table: float32 [32, 12], replicated, may hold values from -4 to 4
- norm2_gain: float32 [768], replicated, may hold values from 0.1 to 1.9
- router: float32 [768, 4], replicated, may hold values from -0.2 to 0.2
- expert_in: bfloat16 [4, 768, 3072], P('expert'), may hold values from -0.21875 to 0.21875
- expert_out: bfloat16 [4, 3072, 768], P('expert'), may hold values from -0.75 to 0.75
- route: int32 [8, 1024], P(('dp', 'expert'), 'context'), may hold values from 0 to 3, as said below
- slot: int32 [8, 1024], P(('dp', 'expert'), 'context'), may hold values from -1 to 79, as said below
- cotangent: bfloat16 [8, 1024, 768], P(('dp', 'expert'), 'context'), may hold values from -6 to 6
Outputs:
- layer_out: bfloat16 [8, 1024, 768], P(('dp', 'expert'), 'context')
- input_grad: bfloat16 [8, 1024, 768], P(('dp', 'expert'), 'context')
- grad_norm1: float32 [768], replicated
- grad_qkv: float32 [768, 2304], P(('dp', 'context'), 'expert')
- grad_wout: float32 [768, 768], P(('dp', 'context'), 'expert')
- grad_bias: float32 [32, 12], replicated
- grad_norm2: float32 [768], replicated
- grad_router: float32 [768, 4], replicated
- grad_expert_in: float32 [4, 768, 3072], P('expert', None, ('dp', 'context'))
- grad_expert_out: float32 [4, 3072, 768], P('expert', ('dp', 'context'))
Inputs may be any that keep to these rules, and one draw needn't show every extreme that they name: `route`: the expert that each token is sent to. `slot`: counted over the rows of one device (its sequences in order, then positions), the tokens sent to one expert hold slots 0, 1, 2, ... in that order up to 79; later ones are dropped and hold -1. In every draw some expert is sent more than 80 tokens of some device, and for each index of dp and of context one expert gets all its 80 slots filled from every device of the expert axis.
All inputs are finite; a program needn't handle non-finite values.
Results may differ from a plain program's by a relative error of at most 0.02.
Values may be sent and summed in bfloat16 or wider, within the bound.
A program may use at most 192 MiB of HBM per device.

v0:
```python
import jax
import jax.numpy as jnp
from jax import lax
from jax.experimental import pallas as pl
from jax.experimental.pallas import tpu as pltpu
from jax.sharding import PartitionSpec as P

D = 768
HEADS = 12
HEAD_DIM = 64
BUCKETS = 32


THRESHOLDS = (12, 16, 23, 32, 46, 64, 91)
SCORE_SCALE = 0.125
EPSILON = 1e-06
HIGHEST = lax.Precision.HIGHEST


def bucket_index(relative):
    distance = jnp.abs(relative)
    far_level = jnp.full_like(distance, 8)
    for threshold in THRESHOLDS:
        far_level = far_level + (distance >= threshold).astype(jnp.int32)
    near_far = jnp.where(distance < 8, distance, far_level)
    return near_far + 16 * (relative > 0).astype(jnp.int32)


def norm_back(grad_normed, values, inverse, gain):
    scaled_grad = grad_normed * gain
    grad_gain = jnp.sum(grad_normed * values * inverse, axis=0)
    grad_values = inverse * scaled_grad - values * inverse**3 * jnp.mean(
        scaled_grad * values, axis=1, keepdims=True
    )
    return (grad_gain, grad_values)


PAIR = 2 * HEAD_DIM
PAIRS = HEADS // 2
GELU_ROOT = 0.7978845608028654
GELU_CUBE = 0.044715


def lane_dot(left, right, left_dim, right_dim):
    return lax.dot_general(
        left, right, (((left_dim,), (right_dim,)), ((), ())), preferred_element_type=jnp.float32
    )


def head_part(block, head):
    lane = lax.broadcasted_iota(jnp.int32, block.shape, 1)
    mine = (lane >= HEAD_DIM) if head else (lane < HEAD_DIM)
    return jnp.where(mine, block, jnp.zeros_like(block))


def forward_kernel(table_ref, q_ref, k_ref, v_ref, out_ref, probs_ref, scores_ref):
    rows = q_ref.shape[0]
    length = k_ref.shape[0]
    blocks = length // rows
    halves = []
    for head in range(2):
        query = head_part(q_ref[...], head)
        peak = None
        for block in range(blocks):
            keys = k_ref[block * rows : (block + 1) * rows, :]
            start = length - (block + 1) * rows
            window = table_ref[0, head : head + 1, start : start + 2 * rows]
            spread = pltpu.roll(
                jnp.broadcast_to(window, (rows, 2 * rows)),
                rows + 1,
                1,
                stride=1,
                stride_axis=0,
            )[:, :rows]
            scores = lane_dot(keys, query, 1, 1) * SCORE_SCALE + spread
            scores_ref[block * rows : (block + 1) * rows, :] = scores
            block_peak = jnp.max(scores, axis=0, keepdims=True)
            peak = block_peak if peak is None else jnp.maximum(peak, block_peak)
        total = jnp.zeros((1, rows), jnp.float32)
        for block in range(blocks):
            part = slice(block * rows, (block + 1) * rows)
            powers = jnp.exp(scores_ref[part, :] - peak)
            scores_ref[part, :] = powers
            total = total + jnp.sum(powers, axis=0, keepdims=True)
        inverse = 1.0 / total
        result = jnp.zeros((rows, PAIR), jnp.float32)
        for block in range(blocks):
            part = slice(block * rows, (block + 1) * rows)
            probs = (scores_ref[part, :] * inverse).astype(jnp.bfloat16)
            probs_ref[head, part, :] = probs
            result = result + lane_dot(probs, v_ref[part, :], 0, 0)
        halves.append(result)
    lane = lax.broadcasted_iota(jnp.int32, (rows, PAIR), 1)
    out_ref[...] = jnp.where(lane < HEAD_DIM, halves[0], halves[1]).astype(out_ref.dtype)


def forward_attention(table, queries, keys_values):
    rows = queries.shape[0]
    length = keys_values.shape[0]
    return pl.pallas_call(
        forward_kernel,
        grid=(PAIRS,),
        in_specs=[
            pl.BlockSpec((1, 8, table.shape[2]), lambda p: (p, 0, 0)),
            pl.BlockSpec((rows, PAIR), lambda p: (0, p)),
            pl.BlockSpec((length, PAIR), lambda p: (0, p)),
            pl.BlockSpec((length, PAIR), lambda p: (0, p + PAIRS)),
        ],
        out_specs=[
            pl.BlockSpec((rows, PAIR), lambda p: (0, p)),
            pl.BlockSpec((2, length, rows), lambda p: (p, 0, 0)),
        ],
        out_shape=[
            jax.ShapeDtypeStruct((rows, D), jnp.bfloat16),
            jax.ShapeDtypeStruct((HEADS, length, rows), jnp.bfloat16),
        ],
        scratch_shapes=[pltpu.VMEM((length, rows), jnp.float32)],
        compiler_params=pltpu.CompilerParams(vmem_limit_bytes=28 * 1024 * 1024),
        cost_estimate=pl.CostEstimate(
            flops=8 * HEADS * rows * length * HEAD_DIM,
            bytes_accessed=2 * HEADS * rows * length + 4 * length * D,
            transcendentals=HEADS * rows * length,
        ),
    )(table, queries, keys_values, keys_values)


def backward_kernel(q_ref, g_ref, k_ref, v_ref, probs_ref, gq_ref, gkv_ref, diag_ref, dp_ref):
    rows = q_ref.shape[0]
    length = k_ref.shape[0]
    blocks = length // rows
    lane_row = lax.broadcasted_iota(jnp.int32, (rows, PAIR), 1)
    query_halves = []
    queries = [head_part(q_ref[...], head) for head in range(2)]
    grads = [head_part(g_ref[...], head) for head in range(2)]
    deltas = []
    for head in range(2):
        delta = jnp.zeros((1, rows), jnp.float32)
        for block in range(blocks):
            part = slice(block * rows, (block + 1) * rows)
            grad_probs = lane_dot(v_ref[part, :], grads[head], 1, 1)
            dp_ref[head, part, :] = grad_probs
            delta = delta + jnp.sum(
                grad_probs * probs_ref[head, part, :].astype(jnp.float32), axis=0, keepdims=True
            )
        deltas.append(delta)
    diag_ref[...] = jnp.zeros_like(diag_ref)
    totals = [jnp.zeros((rows, PAIR), jnp.float32) for head in range(2)]
    for block in range(blocks):
        part = slice(block * rows, (block + 1) * rows)
        start = length - (block + 1) * rows
        grad_keys = jnp.zeros((rows, PAIR), jnp.float32)
        grad_values = jnp.zeros((rows, PAIR), jnp.float32)
        for head in range(2):
            probs = probs_ref[head, part, :]
            grad_scores = probs.astype(jnp.float32) * (dp_ref[head, part, :] - deltas[head])
            low = grad_scores.astype(jnp.bfloat16)
            grad_keys = grad_keys + lane_dot(low, queries[head], 1, 0)
            grad_values = grad_values + lane_dot(probs, grads[head], 1, 0)
            totals[head] = totals[head] + lane_dot(low, k_ref[part, :], 0, 0)
            folded = jnp.zeros((8, 2 * rows), jnp.float32)
            for group in range(rows // 8):
                piece = grad_scores[8 * group : 8 * group + 8, :]
                wide = jnp.concatenate([piece, jnp.zeros_like(piece)], axis=1)
                folded = folded + pltpu.roll(wide, rows - 8 - 8 * group, 1)
            line = jnp.zeros((1, 2 * rows), jnp.float32)
            for sub in range(8):
                row = folded[sub : sub + 1, :]
                line = line + (pltpu.roll(row, 7 - sub, 1) if sub < 7 else row)
            diag_ref[0, head : head + 1, start : start + 2 * rows] += line
        gkv_ref[0, part, :] = (grad_keys * SCORE_SCALE).astype(gkv_ref.dtype)
        gkv_ref[1, part, :] = grad_values.astype(gkv_ref.dtype)
    gq_ref[...] = (jnp.where(lane_row < HEAD_DIM, totals[0], totals[1]) * SCORE_SCALE).astype(
        gq_ref.dtype
    )


def backward_attention(queries, grads, keys_values, probs):
    rows = queries.shape[0]
    length = keys_values.shape[0]
    span = length + rows
    return pl.pallas_call(
        backward_kernel,
        grid=(PAIRS,),
        in_specs=[
            pl.BlockSpec((rows, PAIR), lambda p: (0, p)),
            pl.BlockSpec((rows, PAIR), lambda p: (0, p)),
            pl.BlockSpec((length, PAIR), lambda p: (0, p)),
            pl.BlockSpec((length, PAIR), lambda p: (0, p + PAIRS)),
            pl.BlockSpec((2, length, rows), lambda p: (p, 0, 0)),
        ],
        out_specs=[
            pl.BlockSpec((rows, PAIR), lambda p: (0, p)),
            pl.BlockSpec((2, length, PAIR), lambda p: (0, 0, p)),
            pl.BlockSpec((1, 8, span), lambda p: (p, 0, 0)),
        ],
        out_shape=[
            jax.ShapeDtypeStruct((rows, D), jnp.bfloat16),
            jax.ShapeDtypeStruct((2, length, D), jnp.bfloat16),
            jax.ShapeDtypeStruct((PAIRS, 8, span), jnp.float32),
        ],
        scratch_shapes=[pltpu.VMEM((2, length, rows), jnp.float32)],
        compiler_params=pltpu.CompilerParams(vmem_limit_bytes=28 * 1024 * 1024),
        cost_estimate=pl.CostEstimate(
            flops=20 * HEADS * rows * length * HEAD_DIM,
            bytes_accessed=2 * HEADS * rows * length + 8 * length * D,
            transcendentals=0,
        ),
    )(queries, grads, keys_values, keys_values, probs)


def gelu_both(pre):
    inner = jnp.tanh(GELU_ROOT * (pre + GELU_CUBE * pre * pre * pre))
    half = 0.5 * (1.0 + inner)
    slope = half + 0.5 * pre * (1.0 - inner * inner) * (
        GELU_ROOT * (1.0 + 3.0 * GELU_CUBE * pre * pre)
    )
    return (pre * half, slope)


def expert_hidden(rows, weight_in, weight_out):
    pre = jnp.dot(rows[:, :D], weight_in, preferred_element_type=jnp.float32)
    grad_act = lane_dot(rows[:, D:], weight_out, 1, 1)
    value, slope = gelu_both(pre)
    return (value.astype(jnp.bfloat16), (grad_act * slope).astype(jnp.bfloat16))


def body(
    tokens,
    norm1_gain,
    w_qkv,
    w_out,
    bias_table,
    norm2_gain,
    router,
    expert_in,
    expert_out,
    route,
    slot,
    cotangent,
):
    seqs_here, rows_seq, width = tokens.shape
    contexts = lax.axis_size("context")
    ctx_index = lax.axis_index("context")
    experts_total = router.shape[1]
    tok_rows = seqs_here * rows_seq
    capacity = max(2, 5 * tok_rows // (4 * experts_total))
    query_start = ctx_index * rows_seq
    length = rows_seq * contexts
    weight_in = expert_in[0]
    weight_out = expert_out[0]
    inputs = tokens.astype(jnp.float32).reshape(tok_rows, D)
    grad_out = cotangent.astype(jnp.float32).reshape(tok_rows, D)
    inv_one = lax.rsqrt(jnp.mean(inputs * inputs, axis=1, keepdims=True) + EPSILON)
    normed_one = (inputs * inv_one * norm1_gain).astype(jnp.bfloat16)
    keys_values = lax.all_gather(
        jnp.dot(normed_one, w_qkv[:, D:], preferred_element_type=jnp.float32).astype(jnp.bfloat16),
        "context",
        axis=0,
        tiled=True,
    )
    queries = jnp.dot(normed_one, w_qkv[:, :D], preferred_element_type=jnp.float32).astype(
        jnp.bfloat16
    )
    span = length + rows_seq
    relative = (length - 1 - query_start) - jnp.arange(span, dtype=jnp.int32)
    line_onehot = (
        bucket_index(relative)[None, :] == jnp.arange(BUCKETS, dtype=jnp.int32)[:, None]
    ).astype(jnp.float32)
    line_table = lax.dot_general(
        bias_table, line_onehot, (((0,), (0,)), ((), ())), precision=HIGHEST
    ).reshape(PAIRS, 2, span)
    line_table = jnp.pad(line_table, ((0, 0), (0, 6), (0, 0)))
    attn_low, probs = forward_attention(line_table, queries, keys_values)
    normed_all = lax.all_gather(normed_one, "expert", axis=0, tiled=True)
    attn_all = lax.all_gather(attn_low, "expert", axis=0, tiled=True)
    branch = jnp.dot(attn_low, w_out, preferred_element_type=jnp.float32)
    hidden_sum = inputs + branch
    inv_two = lax.rsqrt(jnp.mean(hidden_sum * hidden_sum, axis=1, keepdims=True) + EPSILON)
    normed_two = hidden_sum * inv_two * norm2_gain
    gates_all = jax.nn.softmax(jnp.dot(normed_two, router, precision=HIGHEST), axis=1)
    routes = route.reshape(tok_rows)
    slots = slot.reshape(tok_rows)
    chosen = (routes[:, None] == jnp.arange(experts_total, dtype=jnp.int32)[None, :]).astype(
        jnp.float32
    )
    gate = jnp.sum(gates_all * chosen, axis=1)
    flat_index = jnp.where(slots >= 0, routes * capacity + slots, -1)
    places = (
        flat_index[:, None] == jnp.arange(experts_total * capacity, dtype=jnp.int32)[None, :]
    ).astype(jnp.bfloat16)
    both_rows = jnp.concatenate(
        [normed_two.astype(jnp.bfloat16), (gate[:, None] * grad_out).astype(jnp.bfloat16)], axis=1
    )
    send_rows = lane_dot(places, both_rows, 0, 0).astype(jnp.bfloat16)
    received = lax.all_to_all(
        send_rows.reshape(experts_total, capacity, 2 * D),
        "expert",
        split_axis=0,
        concat_axis=0,
        tiled=True,
    ).reshape(experts_total * capacity, 2 * D)
    activated, grad_pre = expert_hidden(received, weight_in, weight_out)
    produced = jnp.dot(activated, weight_out, preferred_element_type=jnp.float32)
    grad_sent = lane_dot(grad_pre, weight_in, 1, 1)
    answer = jnp.concatenate([produced, grad_sent], axis=1).astype(jnp.bfloat16)
    answer = lax.all_to_all(
        answer.reshape(experts_total, capacity, 2 * D),
        "expert",
        split_axis=0,
        concat_axis=0,
        tiled=True,
    ).reshape(experts_total * capacity, 2 * D)
    group_rows = lax.all_gather(received, ("dp", "context"), axis=0, tiled=True)
    copies = lax.axis_size("dp") * contexts
    share = weight_in.shape[1] // copies
    first = (lax.axis_index("dp") * contexts + ctx_index) * share
    slice_act, slice_pre = expert_hidden(
        group_rows,
        lax.dynamic_slice_in_dim(weight_in, first, share, axis=1),
        lax.dynamic_slice_in_dim(weight_out, first, share, axis=0),
    )
    grad_in_part = lane_dot(group_rows[:, :D], slice_pre, 0, 0)[None]
    grad_out_part = lane_dot(slice_act, group_rows[:, D:], 0, 0)[None]

    back_rows = jnp.dot(places, answer, preferred_element_type=jnp.float32)
    expert_rows = back_rows[:, :D]
    layer_rows = hidden_sum + gate[:, None] * expert_rows
    layer_out = layer_rows.astype(jnp.bfloat16).reshape(tokens.shape)
    grad_gate = jnp.sum(grad_out * expert_rows, axis=1)
    grad_probs_gate = chosen * grad_gate[:, None]
    grad_logits = gates_all * (
        grad_probs_gate - jnp.sum(gates_all * grad_probs_gate, axis=1, keepdims=True)
    )
    grad_router = jnp.dot(normed_two.T, grad_logits, precision=HIGHEST)
    grad_normed = back_rows[:, D:] + jnp.dot(grad_logits, router.T, precision=HIGHEST)
    grad_norm2, grad_from_norm = norm_back(grad_normed, hidden_sum, inv_two, norm2_gain)
    grad_hidden = grad_out + grad_from_norm
    grad_branch = grad_hidden.astype(jnp.bfloat16)
    grad_attn_low = lane_dot(grad_branch, w_out, 1, 1).astype(jnp.bfloat16)
    grad_q, key_value_terms, diagonals = backward_attention(
        queries, grad_attn_low, keys_values, probs
    )
    grad_table = lax.dot_general(
        line_onehot,
        diagonals[:, :2].reshape(HEADS, span),
        (((1,), (1,)), ((), ())),
        precision=HIGHEST,
    )
    key_value_grad = lax.psum_scatter(key_value_terms, "context", scatter_dimension=1, tiled=True)
    grad_proj = jnp.concatenate([grad_q, key_value_grad[0], key_value_grad[1]], axis=1)
    grad_normed_one = lane_dot(grad_proj, w_qkv, 1, 1)
    grad_norm1, grad_from_first = norm_back(grad_normed_one, inputs, inv_one, norm1_gain)
    input_grad = (grad_hidden + grad_from_first).astype(jnp.bfloat16).reshape(tokens.shape)

    owners = lax.axis_size("expert")
    proj_share = 3 * D // owners
    wout_share = D // owners
    columns = jnp.concatenate(
        [
            grad_proj.reshape(tok_rows, owners, proj_share),
            grad_branch.reshape(tok_rows, owners, wout_share),
        ],
        axis=2,
    )
    columns = lax.all_to_all(
        jnp.transpose(columns, (1, 0, 2)), "expert", split_axis=0, concat_axis=0, tiled=True
    ).reshape(owners * tok_rows, proj_share + wout_share)
    part = jnp.concatenate(
        [
            lane_dot(normed_all, columns[:, :proj_share], 0, 0),
            lane_dot(attn_all, columns[:, proj_share:], 0, 0),
        ],
        axis=1,
    ).astype(jnp.bfloat16)
    part = lax.psum_scatter(
        part, ("dp", "context"), scatter_dimension=0, tiled=True
    ).astype(jnp.float32)
    sum_norm1, sum_table, sum_norm2, sum_router = lax.psum(
        (grad_norm1, grad_table, grad_norm2, grad_router), ("dp", "context", "expert")
    )
    return (
        layer_out,
        input_grad,
        sum_norm1,
        part[:, :proj_share],
        part[:, proj_share:],
        sum_table,
        sum_norm2,
        sum_router,
        grad_in_part,
        grad_out_part,
    )


def solution(mesh):
    in_specs = (
        P(("dp", "expert"), "context", None),
        P(),
        P(),
        P(),
        P(),
        P(),
        P(),
        P("expert", None, None),
        P("expert", None, None),
        P(("dp", "expert"), "context"),
        P(("dp", "expert"), "context"),
        P(("dp", "expert"), "context", None),
    )
    out_specs = (
        P(("dp", "expert"), "context", None),
        P(("dp", "expert"), "context", None),
        P(),
        P(("dp", "context"), "expert"),
        P(("dp", "context"), "expert"),
        P(),
        P(),
        P(),
        P("expert", None, ("dp", "context")),
        P("expert", ("dp", "context"), None),
    )
    return jax.shard_map(body, mesh=mesh, in_specs=in_specs, out_specs=out_specs, check_vma=False)
```

profile of v0, /device:TPU:0, one launch (start us, length us, event | category | flops | bytes accessed | tf_op | source)
XLA Modules:
  0.0 395.3 jit_solution(13472619325809853276)
XLA Ops:
  8.1 1.2 fusion.58
  9.3 0.6 multiply_multiply_fusion.5
  9.9 1.2 fusion.60
  11.1 3.5 convolution_convert_fusion.1
  14.7 0.2 convolution_bitcast_fusion
  15.0 0.6 compare_select_fusion.1
  15.5 1.7 convolution_convert_fusion.4.q_ref
  17.3 28.7 %all-gather.5.cloned.1.call-done.k_ref.v_ref = bf16[1024,1536]{1,0:T(8,128)(2,1)} async-done(((bf16[256,1536]{1,0:T(8,128)(2,1)}), bf16[1024,1536]{1,0:T(8,128)(2,1)}) %all-gather.5.cloned.1.call-update) | async-done | bytes 3145744 | tf_op jit(solution)/shard_map/all_gather | solution.py:255
  46.0 1.9 copy-done.2
  47.9 10.8 %shard_map.195 = (bf16[256,768]{1,0:T(8,128)(2,1)}, bf16[12,1024,256]{2,1,0:T(8,128)(2,1)S(1)}) custom-call(f32[6,8,1280]{2,1,0:T(8,128)S(1)} %pad.4.table_ref, bf16[256,768]{1,0:T(8,128)(2,1)S(1)} %convolution_convert_fusion.4.q_ref, bf16[1024,1536]{1,0:T(8,128)(2,1)S(1)} %copy-done.2, bf16[1024,1536]{1,0:T(8,128)(2,1)S(1)} %copy-done.2), custom_call_target="tpu_custom_call" | custom-call | flops 1610612736 | bytes 9437184 | tf_op jit(solution)/shard_map/pallas_call | solution.py:100
  58.6 2.6 copy-done.4
  61.3 1.6 multiply_reduce_fusion.2
  62.9 0.6 multiply_multiply_fusion.6
  63.5 0.8 fusion.137
  64.4 0.2 fusion.56
  64.6 0.3 copy-done.30
  64.9 1.2 convolution_convert_fusion
  66.1 29.2 %all_to_all.15 = bf16[4,80,1536]{2,1,0:T(8,128)(2,1)} all-to-all(bf16[4,80,1536]{2,1,0:T(8,128)(2,1)S(1)} %bitcast.96), channel_id=1, replica_groups=mesh['dp'=2,'context'=4,'expert'=4] {'expert'}, dimensions={0} | all-to-all | bytes 1966080 | tf_op jit(solution)/shard_map/all_to_all | solution.py:295
  95.4 5.1 %multiply_convert_fusion.1 = (bf16[320,3072]{1,0:T(8,128)(2,1)S(1)}, f32[320,3072]{1,0:T(8,128)S(1)}) fusion(bf16[1,768,3072]{2,1,0:T(8,128)(2,1)} %param.19, bf16[320,1536]{1,0:T(8,128)(2,1)} %bitcast.89), kind=kOutput, calls=%fused_computation.30 | convolution fusion | flops 1518796800 | bytes 11108352 | tf_op jit(solution)/shard_map/dot_general | solution.py:221
  100.5 6.5 %fusion.12 = bf16[320,3072]{1,0:T(8,128)(2,1)S(1)} fusion(bf16[1,3072,768]{2,1,0:T(8,128)(2,1)} %param.20, f32[320,3072]{1,0:T(8,128)S(1)} %get-tuple-element.75, bf16[320,1536]{1,0:T(8,128)(2,1)S(1)} %bitcast.91), kind=kOutput, calls=%fused_computation.15 | convolution fusion | flops 1528627200 | bytes 11108352 | tf_op jit(solution)/shard_map/dot_general | solution.py:45
  107.1 1.8 fusion.52
  108.9 1.7 fusion.49
  110.6 0.1 pad_maximum_fusion.2
  110.7 26.9 %all_to_all.16 = bf16[4,80,1536]{2,1,0:T(8,128)(2,1)S(1)} all-to-all(bf16[4,80,1536]{2,1,0:T(8,128)(2,1)S(1)} %pad_maximum_fusion.2), channel_id=1, replica_groups=mesh['dp'=2,'context'=4,'expert'=4] {'expert'}, dimensions={0} | all-to-all | bytes 1966080 | tf_op jit(solution)/shard_map/all_to_all | solution.py:306
  137.6 0.6 fusion.85
  138.3 0.9 fusion.57
  139.2 1.7 multiply_reduce_fusion
  140.9 1.2 fusion.135
  142.1 0.5 convolution_convert_fusion.3.g_ref
  142.6 13.1 %shard_map.196 = (bf16[256,768]{1,0:T(8,128)(2,1)S(1)}, bf16[2,1024,768]{2,1,0:T(8,128)(2,1)}, f32[6,8,1280]{2,1,0:T(8,128)S(1)}) custom-call(bf16[256,768]{1,0:T(8,128)(2,1)S(1)} %convolution_convert_fusion.4.q_ref, bf16[256,768]{1,0:T(8,128)(2,1)S(1)} %convolution_convert_fusion.3.g_ref, bf16[1024,1536]{1,0:T(8,128)(2,1)S(1)} %copy-done.3, ...), custom_call_target="tpu_custom_call" | custom-call | flops 4026531840 | bytes 12582912 | tf_op jit(solution)/shard_map/pallas_call | solution.py:181
  155.7 0.0 all-gather.7.cloned.1.call-start
  155.8 0.5 all-gather.7.cloned.1.call-update
  156.3 0.9 copy.30
  157.3 34.7 %reduce-scatter.5.cloned.1.call-done = bf16[2,256,768]{2,1,0:T(8,128)(2,1)} async-done(((bf16[2,1024,768]{2,1,0:T(8,128)(2,1)}), bf16[2,256,768]{2,1,0:T(8,128)(2,1)}) %reduce-scatter.5.cloned.1.call-update) | async-done | bytes 786448 | tf_op jit(solution)/shard_map/reduce_scatter | solution.py:349
  192.0 1.2 slice_bitcast_fusion.1
  193.2 0.8 copy-done.11
  194.0 1.1 pad_maximum_fusion
  195.1 1.6 copy.29
  196.6 2.3 maximum_bitcast_fusion
  198.9 4.6 %all-to-all-start.2 = ((bf16[4,256,768]{1,2,0:T(8,128)(2,1)}), bf16[4,256,768]{1,2,0:T(8,128)(2,1)}, u32[]{:S(2)}, u32[]{:S(2)}) async-start(bf16[4,256,768]{1,2,0:T(8,128)(2,1)} %maximum_bitcast_fusion), calls=%async_computation.3 | async-start | bytes 3145728 | tf_op jit(solution)/shard_map/all_to_all | solution.py:365
  203.5 0.6 all-gather.9.cloned.1.call-update
  204.1 61.8 %all-to-all-done.2 = bf16[4,256,768]{1,2,0:T(8,128)(2,1)} async-done(((bf16[4,256,768]{1,2,0:T(8,128)(2,1)}), bf16[4,256,768]{1,2,0:T(8,128)(2,1)}, u32[]{:S(2)}, u32[]{:S(2)}) %all-to-all-start.2) | async-done | bytes 1572896 | tf_op jit(solution)/shard_map/all_to_all | solution.py:365
  265.9 2.6 copy.31
  268.5 3.8 convolution_convert_fusion.2
  272.4 2.3 convolution_convert_fusion.5
  274.8 0.1 pad_maximum_fusion.1
  274.8 1.5 copy.34
  276.3 0.0 all-gather.11.cloned.1.call-start
  276.4 0.7 all-gather.11.cloned.1.call-update
  277.1 0.1 fusion.92
  277.4 0.6 fusion.71
  278.1 3.7 fusion.67
  281.7 38.1 %all-reduce.1 = (f32[768]{0:T(1024)}, f32[32,12]{0,1:T(8,128)}, f32[768]{0:T(1024)}, f32[768,4]{0,1:T(4,128)}) all-reduce(f32[768]{0:T(1024)S(1)} %get-tuple-element.52, f32[32,12]{0,1:T(8,128)S(1)} %fusion.92, f32[768]{0:T(1024)S(1)} %copy-done.25, ...), channel_id=1, replica_groups=mesh['dp'=2,'context'=4,'expert'=4] {'dp','context','expert'}, use_global_device_ids=true, to_apply=%region_11.12 | all-reduce | flops 4992 | bytes 39936 | tf_op jit(solution)/shard_map/psum | solution.py:378
  319.8 1.0 fusion.84
  320.8 1.0 slice.70
  321.8 0.1 copy.36
  321.9 0.9 copy.32
  322.8 0.9 slice.71
  323.7 0.1 copy.37
  323.8 0.7 copy.33
  324.5 39.8 %all-gather.11.cloned.1.call-done = bf16[2560,1536]{1,0:T(8,128)(2,1)} async-done(((bf16[320,1536]{1,0:T(8,128)(2,1)}), bf16[2560,1536]{1,0:T(8,128)(2,1)}) %all-gather.11.cloned.1.call-update) | async-done | bytes 7864336 | tf_op jit(solution)/shard_map/all_gather | solution.py:313
  364.3 6.3 %fusion.32 = f32[2560,384]{1,0:T(8,128)} fusion(bf16[2560,1536]{1,0:T(8,128)(2,1)} %all-gather.11.cloned.1.call-done, bf16[1,768,3072]{2,1,0:T(8,128)(2,1)} %param.19, s32[]{:T(128)S(6)} %select_n.22), kind=kOutput, calls=%fused_computation.37 | convolution fusion | flops 1509949440 | bytes 8454148 | tf_op jit(solution)/shard_map/dot_general | solution.py:221
  370.6 10.7 %fusion.40 = f32[1,768,384]{2,1,0:T(8,128)} fusion(f32[2560,384]{1,0:T(8,128)} %fusion.32, bf16[2560,1536]{1,0:T(8,128)(2,1)} %all-gather.11.cloned.1.call-done, bf16[1,3072,768]{2,1,0:T(8,128)(2,1)} %param.20, s32[]{:T(128)S(6)} %select_n.22), kind=kOutput, calls=%fused_computation.54 | convolution fusion | flops 3038576640 | bytes 13565956 | tf_op jit(solution)/shard_map/dot_general | solution.py:45
  381.3 6.4 %fusion.45 = f32[1,384,768]{2,1,0:T(8,128)} fusion(bf16[2560,1536]{1,0:T(8,128)(2,1)} %all-gather.11.cloned.1.call-done, f32[2560,384]{1,0:T(8,128)} %fusion.32), kind=kOutput, calls=%fused_computation.55 | convolution fusion | flops 1518796800 | bytes 9043968 | tf_op jit(solution)/shard_map/dot_general | solution.py:45
  (105 shorter events, 0.6 us)
Async XLA Ops:
  8.0 53.3 %copy-start = (bf16[768,768]{1,0:T(8,128)(2,1)S(1)}, bf16[768,768]{1,0:T(8,128)(2,1)}, u32[]{:S(2)}) copy-start(bf16[768,768]{1,0:T(8,128)(2,1)} %param.15) | copy-start | bytes 3538948
  8.0 6.6 %copy-start.32 = (f32[32,12]{0,1:T(8,128)S(1)}, f32[32,12]{0,1:T(8,128)}, u32[]{:S(2)}) copy-start(f32[32,12]{0,1:T(8,128)} %param.16) | copy-start | bytes 4612
  8.0 6.9 %copy-start.19 = (s32[1,256]{1,0:T(1,128)S(1)}, s32[1,256]{1,0:T(1,128)}, u32[]{:S(2)}) copy-start(s32[1,256]{1,0:T(1,128)} %param.21) | copy-start | bytes 3076
  8.0 6.9 %copy-start.36 = (s32[1,256]{1,0:T(1,128)S(1)}, s32[1,256]{1,0:T(1,128)}, u32[]{:S(2)}) copy-start(s32[1,256]{1,0:T(1,128)} %param.22) | copy-start | bytes 3076
  8.1 37.9 %all-gather.5.cloned.1.call-start = ((), (), s32[]{:S(2)}) async-start(), calls=%async_computation.5 | async-start | bytes 3932160 | tf_op jit(solution)/shard_map/all_gather | solution.py:255
  9.9 4.7 %copy-start.26 = (f32[256]{0:T(256)}, f32[256]{0:T(256)S(1)}, u32[]{:S(2)}) copy-start(f32[256]{0:T(256)S(1)} %get-tuple-element.67) | copy-start | bytes 3076
  11.1 6.2 %copy-start.9 = (bf16[256,768]{1,0:T(8,128)(2,1)}, bf16[256,768]{1,0:T(8,128)(2,1)S(1)}, u32[]{:S(2)}) copy-start(bf16[256,768]{1,0:T(8,128)(2,1)S(1)} %fusion.60) | copy-start | bytes 1179652
  14.6 177.4 %reduce-scatter.5.cloned.1.call-start = ((), (), s32[]{:S(2)}) async-start(), calls=%async_computation.6 | async-start | bytes 3932160 | tf_op jit(solution)/shard_map/reduce_scatter | solution.py:349
  46.0 1.9 copy-start.2
  47.9 13.4 %copy-start.5 = (bf16[1,256,768]{2,1,0:T(8,128)(2,1)S(1)}, bf16[1,256,768]{2,1,0:T(8,128)(2,1)}, u32[]{:S(2)}) copy-start(bf16[1,256,768]{2,1,0:T(8,128)(2,1)} %param.12) | copy-start | bytes 1179652
  47.9 15.6 %copy-start.13 = (f32[768]{0:T(1024)S(1)}, f32[768]{0:T(1024)}, u32[]{:S(2)}) copy-start(f32[768]{0:T(1024)} %param.17) | copy-start | bytes 9220
  47.9 15.6 %copy-start.14 = (f32[768,4]{0,1:T(4,128)S(1)}, f32[768,4]{0,1:T(4,128)}, u32[]{:S(2)}) copy-start(f32[768,4]{0,1:T(4,128)} %param.18) | copy-start | bytes 36868
  47.9 16.5 %copy-start.7 = (bf16[1,256,768]{2,1,0:T(8,128)(2,1)S(1)}, bf16[1,256,768]{2,1,0:T(8,128)(2,1)}, u32[]{:S(2)}) copy-start(bf16[1,256,768]{2,1,0:T(8,128)(2,1)} %param.23) | copy-start | bytes 1179652
  58.6 2.6 copy-start.4
  63.4 1.1 copy-start.16
  64.4 0.6 copy-start.30
  95.4 5.1 %copy-start.6 = (bf16[4,80,1536]{2,1,0:T(8,128)(2,1)S(1)}, bf16[4,80,1536]{2,1,0:T(8,128)(2,1)}, u32[]{:S(2)}) copy-start(bf16[4,80,1536]{2,1,0:T(8,128)(2,1)} %all_to_all.15) | copy-start | bytes 2949124
  95.4 11.7 %slice-start.2 = ((s8[4718592]{0:T(1024)(128)(4,1)}), s8[4194304]{0:T(1024)(128)(4,1)S(1)}, s32[]{:S(2)}) async-start(s8[4718592]{0:T(1024)(128)(4,1)} %bitcast.103), calls=%async_computation.13 | async-start | bytes 8388608
  95.4 13.5 %slice-start.4 = ((s8[4718592]{0:T(1024)(128)(4,1)}), s8[4194304]{0:T(1024)(128)(4,1)S(1)}, s32[]{:S(2)}) async-start(s8[4718592]{0:T(1024)(128)(4,1)} %bitcast.105), calls=%async_computation.15 | async-start | bytes 8388608
  100.5 6.6 %slice-start.3 = ((s8[4718592]{0:T(1024)(128)(4,1)}), s8[524288]{0:T(1024)(128)(4,1)S(1)}, s32[]{:S(2)}) async-start(s8[4718592]{0:T(1024)(128)(4,1)} %bitcast.103), calls=%async_computation.14 | async-start | bytes 1048576
  100.5 8.3 %slice-start.5 = ((s8[4718592]{0:T(1024)(128)(4,1)}), s8[524288]{0:T(1024)(128)(4,1)S(1)}, s32[]{:S(2)}) async-start(s8[4718592]{0:T(1024)(128)(4,1)} %bitcast.105), calls=%async_computation.16 | async-start | bytes 1048576
  108.9 33.7 %slice-start = ((s8[6291456]{0:T(1024)(128)(4,1)}), s8[4194304]{0:T(1024)(128)(4,1)S(1)}, s32[]{:S(2)}) async-start(s8[6291456]{0:T(1024)(128)(4,1)} %bitcast.86), calls=%async_computation.11 | async-start | bytes 8388608
  110.6 27.0 %copy-start.35 = (s32[256]{0:T(256)S(1)}, s32[256]{0:T(256)}, u32[]{:S(2)}) copy-start(s32[256]{0:T(256)} %compare_select_fusion.1) | copy-start | bytes 3076
  110.6 27.7 %copy-start.31 = (f32[256]{0:T(256)S(1)}, f32[256]{0:T(256)}, u32[]{:S(2)}) copy-start(f32[256]{0:T(256)} %copy-done.30) | copy-start | bytes 3076
  110.7 28.5 %copy-start.20 = (s32[1,256]{1,0:T(1,128)S(1)}, s32[1,256]{1,0:T(1,128)}, u32[]{:S(2)}) copy-start(s32[1,256]{1,0:T(1,128)} %param.21) | copy-start | bytes 3076
  110.7 28.5 %copy-start.15 = (f32[768,4]{0,1:T(4,128)S(1)}, f32[768,4]{0,1:T(4,128)}, u32[]{:S(2)}) copy-start(f32[768,4]{0,1:T(4,128)} %param.18) | copy-start | bytes 36868
  110.7 28.5 %copy-start.17 = (f32[256]{0:T(256)S(1)}, f32[256]{0:T(256)}, u32[]{:S(2)}) copy-start(f32[256]{0:T(256)} %copy-done.16) | copy-start | bytes 3076
  110.7 31.9 %slice-start.1 = ((s8[6291456]{0:T(1024)(128)(4,1)}), s8[2097152]{0:T(1024)(128)(4,1)S(1)}, s32[]{:S(2)}) async-start(s8[6291456]{0:T(1024)(128)(4,1)} %bitcast.86), calls=%async_computation.12 | async-start | bytes 4194304
  137.6 3.3 copy-start.34
  139.2 3.4 copy-start.23
  139.2 3.4 copy-start.3
  139.2 3.4 copy-start.28
  155.7 112.8 %all-gather.7.cloned.1.call-start = ((), (), s32[]{:S(2)}) async-start(), calls=%async_computation.7 | async-start | bytes 1966080 | tf_op jit(solution)/shard_map/all_gather | solution.py:274
  193.2 0.8 copy-start.11
  193.2 5.7 %copy-start.10 = (bf16[256,768]{1,0:T(8,128)(2,1)}, bf16[256,768]{1,0:T(8,128)(2,1)S(1)}, u32[]{:S(2)}) copy-start(bf16[256,768]{1,0:T(8,128)(2,1)S(1)} %get-tuple-element.64) | copy-start | bytes 1179652
  198.9 67.0 %all-to-all-start.2 = ((bf16[4,256,768]{1,2,0:T(8,128)(2,1)}), bf16[4,256,768]{1,2,0:T(8,128)(2,1)}, u32[]{:S(2)}, u32[]{:S(2)}) async-start(bf16[4,256,768]{1,2,0:T(8,128)(2,1)} %maximum_bitcast_fusion), calls=%async_computation.3 | async-start | bytes 3145728 | tf_op jit(solution)/shard_map/all_to_all | solution.py:365
  203.5 68.8 %all-gather.9.cloned.1.call-start = ((), (), s32[]{:S(2)}) async-start(), calls=%async_computation.8 | async-start | bytes 1966080 | tf_op jit(solution)/shard_map/all_gather | solution.py:275
  204.1 116.7 %reduce-scatter.7.cloned.1.call-start = ((), (), s32[]{:S(2)}) async-start(), calls=%async_computation.10 | async-start | bytes 1327104
  272.4 2.4 copy-start.12
  274.7 2.6 copy-start.18
  274.7 2.6 copy-start.21
  274.7 2.6 copy-start.24
  274.7 2.6 copy-start.29
  276.3 88.0 %all-gather.11.cloned.1.call-start = ((), (), s32[]{:S(2)}) async-start(), calls=%async_computation.9 | async-start | bytes 8847360 | tf_op jit(solution)/shard_map/all_gather | solution.py:313
  278.0 3.8 copy-start.25
  278.0 41.8 %copy-start.8 = (f32[256,768]{1,0:T(8,128)S(1)}, f32[256,768]{1,0:T(8,128)}, u32[]{:S(2)}) copy-start(f32[256,768]{1,0:T(8,128)} %get-tuple-element.59) | copy-start | bytes 2359300
  278.0 41.8 %copy-start.22 = (f32[768]{0:T(1024)S(1)}, f32[768]{0:T(1024)}, u32[]{:S(2)}) copy-start(f32[768]{0:T(1024)} %param.13) | copy-start | bytes 9220
  278.0 41.8 %copy-start.27 = (f32[256]{0:T(256)S(1)}, f32[256]{0:T(256)}, u32[]{:S(2)}) copy-start(f32[256]{0:T(256)} %copy-done.26) | copy-start | bytes 3076
  278.0 41.8 %copy-start.33 = (f32[256]{0:T(256)S(1)}, f32[256]{0:T(256)}, u32[]{:S(2)}) copy-start(f32[256]{0:T(256)} %get-tuple-element.66) | copy-start | bytes 3076
  381.3 6.4 %copy-start.1 = (bf16[768,768]{1,0:T(8,128)(2,1)S(1)}, bf16[768,768]{1,0:T(8,128)(2,1)}, u32[]{:S(2)}) copy-start(bf16[768,768]{1,0:T(8,128)(2,1)} %param.15) | copy-start | bytes 3538948
Sparse Core Ops, SparseCore 0:
  14.7 31.2 all-gather.4
  155.9 36.0 reduce-scatter.4
Sparse Core Ops, SparseCore 1:
  157.9 35.0 all-gather.6
  206.2 58.6 all-gather.8
  276.4 33.9 reduce-scatter.6
  312.2 52.0 all-gather.10
where the time goes:
time: 396 us; the launch traced here: 395 us
  waiting for transfers between devices  167 us (42%)
  blocking collectives  94.2 us (24%)
  matrix products  60.8 us (15%)
  Pallas kernels  23.9 us (6%)
  local copies, waits for them, and re-layouts  17.4 us (4%)
  between operations  16.4 us (4%)
  other arithmetic  11 us (3%)
  starting transfers between devices  4.82 us (1%)
    all_to_all x1, waiting for transfers between devices, body(): lax.all_to_all(jnp.transpose(columns, (1, 0, 2)), 'expert', split_axis=0,...  61.8 us
    all_gather x1, waiting for transfers between devices, body(): group_rows = lax.all_gather(received, ('dp', 'context'), axis=0, tiled=True)  39.8 us
    psum x1, blocking collectives, body(): lax.psum((grad_norm1, grad_table, grad_norm2, grad_router), ('dp', 'conte...  38.1 us
    dot_general x9, matrix products, lane_dot(): lax.dot_general(left, right, (((left_dim,), (right_dim,)), ((), ())), pre...  36.9 us
    reduce_scatter x1, waiting for transfers between devices, body(): lax.psum_scatter(key_value_terms, 'context', scatter_dimension=1, tiled=T...  34.7 us
    all_to_all x1, blocking collectives, body(): lax.all_to_all(send_rows.reshape(experts_total, capacity, 2 * D), 'expert...  29.2 us
    all_gather x1, waiting for transfers between devices, body(): lax.all_gather(jnp.dot(normed_one, w_qkv[:, D:], preferred_element_type=j...  28.7 us
    all_to_all x1, blocking collectives, body(): lax.all_to_all(answer.reshape(experts_total, capacity, 2 * D), 'expert',...  26.9 us
  transfers between devices with their start and end apart: 7, of which 4 were waited for; matrix products, arithmetic and copies ran while one was open for 6% of the time, Pallas kernels for 0%

commit v1 on v0

--- a/solution.py
+++ b/solution.py
@@ -124,7 +124,7 @@
     )(table, queries, keys_values, keys_values)
 
 
-def backward_kernel(q_ref, g_ref, k_ref, v_ref, probs_ref, gq_ref, gkv_ref, diag_ref, dp_ref):
+def backward_kernel(q_ref, g_ref, k_ref, v_ref, probs_ref, gq_ref, gk_ref, gv_ref, diag_ref, dp_ref):
     rows = q_ref.shape[0]
     length = k_ref.shape[0]
     blocks = length // rows
@@ -167,8 +167,8 @@
                 row = folded[sub : sub + 1, :]
                 line = line + (pltpu.roll(row, 7 - sub, 1) if sub < 7 else row)
             diag_ref[0, head : head + 1, start : start + 2 * rows] += line
-        gkv_ref[0, part, :] = (grad_keys * SCORE_SCALE).astype(gkv_ref.dtype)
-        gkv_ref[1, part, :] = grad_values.astype(gkv_ref.dtype)
+        gk_ref[part, :] = (grad_keys * SCORE_SCALE).astype(gk_ref.dtype)
+        gv_ref[part, :] = grad_values.astype(gv_ref.dtype)
     gq_ref[...] = (jnp.where(lane_row < HEAD_DIM, totals[0], totals[1]) * SCORE_SCALE).astype(
         gq_ref.dtype
     )
@@ -190,12 +190,14 @@
         ],
         out_specs=[
             pl.BlockSpec((rows, PAIR), lambda p: (0, p)),
-            pl.BlockSpec((2, length, PAIR), lambda p: (0, 0, p)),
+            pl.BlockSpec((length, PAIR), lambda p: (0, p)),
+            pl.BlockSpec((length, PAIR), lambda p: (0, p)),
             pl.BlockSpec((1, 8, span), lambda p: (p, 0, 0)),
         ],
         out_shape=[
             jax.ShapeDtypeStruct((rows, D), jnp.bfloat16),
-            jax.ShapeDtypeStruct((2, length, D), jnp.bfloat16),
+            jax.ShapeDtypeStruct((length, D), jnp.bfloat16),
+            jax.ShapeDtypeStruct((length, D), jnp.bfloat16),
             jax.ShapeDtypeStruct((PAIRS, 8, span), jnp.float32),
         ],
         scratch_shapes=[pltpu.VMEM((2, length, rows), jnp.float32)],
@@ -252,11 +254,9 @@
     grad_out = cotangent.astype(jnp.float32).reshape(tok_rows, D)
     inv_one = lax.rsqrt(jnp.mean(inputs * inputs, axis=1, keepdims=True) + EPSILON)
     normed_one = (inputs * inv_one * norm1_gain).astype(jnp.bfloat16)
-    keys_values = lax.all_gather(
-        jnp.dot(normed_one, w_qkv[:, D:], preferred_element_type=jnp.float32).astype(jnp.bfloat16),
-        "context",
-        axis=0,
-        tiled=True,
+    normed_seq = lax.all_gather(normed_one, "context", axis=0, tiled=True)
+    keys_values = jnp.dot(normed_seq, w_qkv[:, D:], preferred_element_type=jnp.float32).astype(
+        jnp.bfloat16
     )
     queries = jnp.dot(normed_one, w_qkv[:, :D], preferred_element_type=jnp.float32).astype(
         jnp.bfloat16
@@ -271,8 +271,6 @@
     ).reshape(PAIRS, 2, span)
     line_table = jnp.pad(line_table, ((0, 0), (0, 6), (0, 0)))
     attn_low, probs = forward_attention(line_table, queries, keys_values)
-    normed_all = lax.all_gather(normed_one, "expert", axis=0, tiled=True)
-    attn_all = lax.all_gather(attn_low, "expert", axis=0, tiled=True)
     branch = jnp.dot(attn_low, w_out, preferred_element_type=jnp.float32)
     hidden_sum = inputs + branch
     inv_two = lax.rsqrt(jnp.mean(hidden_sum * hidden_sum, axis=1, keepdims=True) + EPSILON)
@@ -299,6 +297,7 @@
         concat_axis=0,
         tiled=True,
     ).reshape(experts_total * capacity, 2 * D)
+    group_rows = lax.all_gather(received, ("dp", "context"), axis=0, tiled=True)
     activated, grad_pre = expert_hidden(received, weight_in, weight_out)
     produced = jnp.dot(activated, weight_out, preferred_element_type=jnp.float32)
     grad_sent = lane_dot(grad_pre, weight_in, 1, 1)
@@ -310,18 +309,6 @@
         concat_axis=0,
         tiled=True,
     ).reshape(experts_total * capacity, 2 * D)
-    group_rows = lax.all_gather(received, ("dp", "context"), axis=0, tiled=True)
-    copies = lax.axis_size("dp") * contexts
-    share = weight_in.shape[1] // copies
-    first = (lax.axis_index("dp") * contexts + ctx_index) * share
-    slice_act, slice_pre = expert_hidden(
-        group_rows,
-        lax.dynamic_slice_in_dim(weight_in, first, share, axis=1),
-        lax.dynamic_slice_in_dim(weight_out, first, share, axis=0),
-    )
-    grad_in_part = lane_dot(group_rows[:, :D], slice_pre, 0, 0)[None]
-    grad_out_part = lane_dot(slice_act, group_rows[:, D:], 0, 0)[None]
-
     back_rows = jnp.dot(places, answer, preferred_element_type=jnp.float32)
     expert_rows = back_rows[:, :D]
     layer_rows = hidden_sum + gate[:, None] * expert_rows
@@ -337,7 +324,9 @@
     grad_hidden = grad_out + grad_from_norm
     grad_branch = grad_hidden.astype(jnp.bfloat16)
     grad_attn_low = lane_dot(grad_branch, w_out, 1, 1).astype(jnp.bfloat16)
-    grad_q, key_value_terms, diagonals = backward_attention(
+    grad_attn_low, group_rows = lax.optimization_barrier((grad_attn_low, group_rows))
+    grad_wout = lane_dot(attn_low, grad_branch, 0, 0).astype(jnp.bfloat16)
+    grad_q, key_terms, value_terms, diagonals = backward_attention(
         queries, grad_attn_low, keys_values, probs
     )
     grad_table = lax.dot_general(
@@ -346,35 +335,51 @@
         (((1,), (1,)), ((), ())),
         precision=HIGHEST,
     )
-    key_value_grad = lax.psum_scatter(key_value_terms, "context", scatter_dimension=1, tiled=True)
-    grad_proj = jnp.concatenate([grad_q, key_value_grad[0], key_value_grad[1]], axis=1)
-    grad_normed_one = lane_dot(grad_proj, w_qkv, 1, 1)
+    normed_terms = lane_dot(key_terms, w_qkv[:, D : 2 * D], 1, 1) + lane_dot(
+        value_terms, w_qkv[:, 2 * D :], 1, 1
+    )
+    normed_terms, grad_q, key_terms, value_terms = lax.optimization_barrier(
+        (normed_terms.astype(jnp.bfloat16), grad_q, key_terms, value_terms)
+    )
+    copies = lax.axis_size("dp") * contexts
+    share = weight_in.shape[1] // copies
+    first = (lax.axis_index("dp") * contexts + ctx_index) * share
+    slice_act, slice_pre = expert_hidden(
+        group_rows,
+        lax.dynamic_slice_in_dim(weight_in, first, share, axis=1),
+        lax.dynamic_slice_in_dim(weight_out, first, share, axis=0),
+    )
+    summed_terms = lax.psum_scatter(normed_terms, "context", scatter_dimension=0, tiled=True)
+    summed_terms, slice_act, slice_pre = lax.optimization_barrier(
+        (summed_terms, slice_act, slice_pre)
+    )
+    grad_normed_one = summed_terms.astype(jnp.float32) + lane_dot(grad_q, w_qkv[:, :D], 1, 1)
     grad_norm1, grad_from_first = norm_back(grad_normed_one, inputs, inv_one, norm1_gain)
     input_grad = (grad_hidden + grad_from_first).astype(jnp.bfloat16).reshape(tokens.shape)
 
+    grad_in_part = lane_dot(group_rows[:, :D], slice_pre, 0, 0)[None]
+    grad_out_part = lane_dot(slice_act, group_rows[:, D:], 0, 0)[None]
+
     owners = lax.axis_size("expert")
     proj_share = 3 * D // owners
-    wout_share = D // owners
-    columns = jnp.concatenate(
+    grad_both = jnp.concatenate(
         [
-            grad_proj.reshape(tok_rows, owners, proj_share),
-            grad_branch.reshape(tok_rows, owners, wout_share),
-        ],
-        axis=2,
-    )
-    columns = lax.all_to_all(
-        jnp.transpose(columns, (1, 0, 2)), "expert", split_axis=0, concat_axis=0, tiled=True
-    ).reshape(owners * tok_rows, proj_share + wout_share)
+            lane_dot(normed_one, grad_q, 0, 0).astype(jnp.bfloat16),
+            lane_dot(normed_seq, key_terms, 0, 0).astype(jnp.bfloat16),
+            lane_dot(normed_seq, value_terms, 0, 0).astype(jnp.bfloat16),
+            grad_wout,
+        ],
+        axis=1,
+    )
+    part_both = lax.psum_scatter(grad_both, ("dp", "context"), scatter_dimension=0, tiled=True)
+    part_qkv, part_wout = part_both[:, : 3 * D], part_both[:, 3 * D :]
+    rows_here = part_both.shape[0]
     part = jnp.concatenate(
-        [
-            lane_dot(normed_all, columns[:, :proj_share], 0, 0),
-            lane_dot(attn_all, columns[:, proj_share:], 0, 0),
-        ],
-        axis=1,
-    ).astype(jnp.bfloat16)
+        [part_qkv.reshape(rows_here, owners, -1), part_wout.reshape(rows_here, owners, -1)], axis=2
+    )
     part = lax.psum_scatter(
-        part, ("dp", "context"), scatter_dimension=0, tiled=True
-    ).astype(jnp.float32)
+        jnp.transpose(part, (1, 0, 2)), "expert", scatter_dimension=0, tiled=True
+    )[0].astype(jnp.float32)
     sum_norm1, sum_table, sum_norm2, sum_router = lax.psum(
         (grad_norm1, grad_table, grad_norm2, grad_router), ("dp", "context", "expert")
     )

time: 396 us -> 311 us (0.79); the launches traced: 395 us -> 305 us
  waiting for transfers between devices: 167 us -> 73.7 us
  matrix products: 60.8 us -> 64.9 us
    all_to_all x1 -> x0, waiting for transfers between devices: 61.8 us -> none  [body(): lax.all_to_all(jnp.transpose(columns, (1, 0, 2)), 'expert', split_axis=0,...]
    unnamed x7 -> x6, waiting for transfers between devices: 1.81 us -> 53.1 us
    all_gather x1, waiting for transfers between devices: 39.8 us -> 2.26 us  [body(): group_rows = lax.all_gather(received, ('dp', 'context'), axis=0, tiled=True)]
    reduce_scatter x1 -> x2, waiting for transfers between devices: 34.7 us -> 0.01 us  [the longest x1 0.01 us: body(): lax.psum_scatter(normed_terms, 'context', scatter_dimension=0, tiled=True)]
    all_gather x3 -> x1, waiting for transfers between devices: 28.7 us -> 18.3 us  [body(): normed_seq = lax.all_gather(normed_one, 'context', axis=0, tiled=True)]
    unnamed x91 -> x99, local copies, waits for them, and re-layouts: 9.19 us -> 14.3 us
    all_to_all x1 -> x0, starting transfers between devices: 4.61 us -> none  [body(): lax.all_to_all(jnp.transpose(columns, (1, 0, 2)), 'expert', split_axis=0,...]
    dot_general x9 -> x14, matrix products: 36.9 us -> 39.8 us  [lane_dot(): lax.dot_general(left, right, (((left_dim,), (right_dim,)), ((), ())), pre...]
  transfers between devices with their start and end apart: 7 -> 5, of which waited for: 4 -> 3; matrix products, arithmetic and copies ran while one was open for 6% -> 22% of each run, Pallas kernels for 0% -> 0%
where the time goes in v1:
time: 311 us; the launch traced here: 305 us
  blocking collectives  96.7 us (31%)
  waiting for transfers between devices  73.7 us (24%)
  matrix products  64.9 us (21%)
  Pallas kernels  22.9 us (7%)
  local copies, waits for them, and re-layouts  18.3 us (6%)
  between operations  14.8 us (5%)
  other arithmetic  12.9 us (4%)
    unnamed x6, waiting for transfers between devices  53.1 us
    psum x1, blocking collectives, body(): lax.psum((grad_norm1, grad_table, grad_norm2, grad_router), ('dp', 'conte...  40.5 us
    dot_general x14, matrix products, lane_dot(): lax.dot_general(left, right, (((left_dim,), (right_dim,)), ((), ())), pre...  39.8 us
    all_to_all x1, blocking collectives, body(): lax.all_to_all(send_rows.reshape(experts_total, capacity, 2 * D), 'expert...  29.2 us
    all_to_all x1, blocking collectives, body(): lax.all_to_all(answer.reshape(experts_total, capacity, 2 * D), 'expert',...  27 us
    all_gather x1, waiting for transfers between devices, body(): normed_seq = lax.all_gather(normed_one, 'context', axis=0, tiled=True)  18.3 us
    unnamed x99, local copies, waits for them, and re-layouts  14.3 us
    pallas_call x1, Pallas kernels, backward_attention(): pl.pallas_call(backward_kernel, grid=(PAIRS,), in_specs=[pl.BlockSpec((ro...  12.7 us
  transfers between devices with their start and end apart: 5, of which 3 were waited for; matrix products, arithmetic and copies ran while one was open for 22% of the time, Pallas kernels for 0%

profile of v1, /device:TPU:0, one launch (start us, length us, event | category | flops | bytes accessed | tf_op | source)
XLA Modules:
  0.0 305.1 jit_solution(15816558275304184762)
XLA Ops:
  7.2 1.2 fusion.54
  8.5 0.6 multiply_multiply_fusion.5
  9.1 1.9 fusion.56
  11.1 0.9 convolution_bitcast_fusion
  12.0 1.3 compare_select_fusion.1
  13.3 1.9 convolution_convert_fusion.7.q_ref
  15.2 18.3 %all-gather.3.cloned.1.call-done = bf16[1024,768]{1,0:T(8,128)(2,1)} async-done(((bf16[256,768]{1,0:T(8,128)(2,1)}), bf16[1024,768]{1,0:T(8,128)(2,1)}) %all-gather.3.cloned.1.call-update) | async-done | bytes 1572880 | tf_op jit(solution)/shard_map/all_gather | solution.py:257
  33.5 4.7 %convolution_convert_fusion.k_ref.v_ref = bf16[1024,1536]{1,0:T(8,128)(2,1)S(1)} fusion(bf16[1024,768]{1,0:T(8,128)(2,1)} %all-gather.3.cloned.1.call-done, bf16[768,2304]{1,0:T(8,128)(2,1)} %param.14), kind=kOutput, calls=%fused_computation.33 | convolution fusion | flops 2417491968 | bytes 7077888 | tf_op jit(solution)/shard_map/dot_general | solution.py:258
  38.3 10.2 %shard_map.195 = (bf16[256,768]{1,0:T(8,128)(2,1)S(1)}, bf16[12,1024,256]{2,1,0:T(8,128)(2,1)S(1)}) custom-call(f32[6,8,1280]{2,1,0:T(8,128)S(1)} %pad.4.table_ref, bf16[256,768]{1,0:T(8,128)(2,1)S(1)} %convolution_convert_fusion.7.q_ref, bf16[1024,1536]{1,0:T(8,128)(2,1)S(1)} %convolution_convert_fusion.k_ref.v_ref, ...), custom_call_target="tpu_custom_call" | custom-call | flops 1610612736 | bytes 9437184 | tf_op jit(solution)/shard_map/pallas_call | solution.py:100
  48.5 0.6 multiply_reduce_fusion.2
  49.1 1.0 multiply_multiply_fusion.6
  50.1 0.8 fusion.120
  51.0 0.2 fusion.52
  51.2 0.3 copy-done.35
  51.6 0.5 convolution_convert_fusion.1
  52.1 29.2 %all_to_all.10 = bf16[4,80,1536]{2,1,0:T(8,128)(2,1)} all-to-all(bf16[4,80,1536]{2,1,0:T(8,128)(2,1)S(1)} %bitcast.97), channel_id=1, replica_groups=mesh['dp'=2,'context'=4,'expert'=4] {'expert'}, dimensions={0} | all-to-all | bytes 1966080 | tf_op jit(solution)/shard_map/all_to_all | solution.py:293
  81.4 0.6 reduce-scatter.6.cloned.1.call-start
  82.0 5.1 %multiply_convert_fusion.1 = (bf16[320,3072]{1,0:T(8,128)(2,1)S(1)}, f32[320,3072]{1,0:T(8,128)S(1)}) fusion(bf16[1,768,3072]{2,1,0:T(8,128)(2,1)} %param.19, bf16[320,1536]{1,0:T(8,128)(2,1)} %bitcast.93), kind=kOutput, calls=%fused_computation.31 | convolution fusion | flops 1518796800 | bytes 11108352 | tf_op jit(solution)/shard_map/dot_general | solution.py:223
  87.1 6.9 %fusion.12 = bf16[320,3072]{1,0:T(8,128)(2,1)S(1)} fusion(bf16[1,3072,768]{2,1,0:T(8,128)(2,1)} %param.20, f32[320,3072]{1,0:T(8,128)S(1)} %get-tuple-element.61, bf16[320,1536]{1,0:T(8,128)(2,1)S(1)} %bitcast.94), kind=kOutput, calls=%fused_computation.16 | convolution fusion | flops 1528627200 | bytes 11108352 | tf_op jit(solution)/shard_map/dot_general | solution.py:45
  94.1 1.8 fusion.44
  95.9 1.7 fusion.41
  97.6 0.1 pad_maximum_fusion.1
  97.7 27.0 %all_to_all.11 = bf16[4,80,1536]{2,1,0:T(8,128)(2,1)S(1)} all-to-all(bf16[4,80,1536]{2,1,0:T(8,128)(2,1)S(1)} %pad_maximum_fusion.1), channel_id=1, replica_groups=mesh['dp'=2,'context'=4,'expert'=4] {'expert'}, dimensions={0} | all-to-all | bytes 1966080 | tf_op jit(solution)/shard_map/all_to_all | solution.py:305
  124.7 0.6 fusion.78
  125.3 0.9 fusion.53
  126.3 1.6 multiply_reduce_fusion
  127.9 0.2 convert_add_fusion.1
  128.2 0.9 copy-done.12
  129.1 0.5 convolution_convert_fusion.6.g_ref
  129.6 2.3 all-gather.5.cloned.1.call-done
  131.8 1.9 copy-done.3
  133.7 2.8 copy-done.5
  136.5 12.7 %shard_map.196 = (bf16[256,768]{1,0:T(8,128)(2,1)S(1)}, bf16[1024,768]{1,0:T(8,128)(2,1)S(1)}, bf16[1024,768]{1,0:T(8,128)(2,1)S(1)}, f32[6,8,1280]{2,1,0:T(8,128)S(1)}) custom-call(bf16[256,768]{1,0:T(8,128)(2,1)S(1)} %convolution_convert_fusion.7.q_ref, bf16[256,768]{1,0:T(8,128)(2,1)S(1)} %convolution_convert_fusion.6.g_ref, ...), custom_call_target="tpu_custom_call" | custom-call | flops 4026531840 | bytes 12582912 | tf_op jit(solution)/shard_map/pallas_call | solution.py:181
  149.3 1.4 fusion.48
  150.7 0.3 copy-done.6
  151.0 2.6 add_convert_fusion
  153.7 1.8 convolution_convert_fusion.2
  155.5 0.5 convolution_convert_fusion.5
  156.0 1.5 convolution_convert_fusion.3
  157.5 1.5 convolution_convert_fusion.4
  159.1 2.5 pad_maximum_fusion
  161.5 6.7 %copy.26 = bf16[768,3072]{1,0:T(8,128)(2,1)} copy(bf16[768,3072]{0,1:T(8,128)(2,1)} %pad_maximum_fusion) | data formatting | bytes 9437184
  168.3 0.3 reduce-scatter.8.cloned.1.call-start
  168.6 0.8 copy-done.11
  169.4 0.6 fusion.67
  170.1 0.1 fusion.87
  170.2 6.5 %multiply_convert_fusion = (bf16[2560,384]{1,0:T(8,128)(2,1)}, f32[2560,384]{1,0:T(8,128)S(1)}) fusion(bf16[1,768,3072]{2,1,0:T(8,128)(2,1)} %param.19, s32[]{:T(128)S(6)} %select_n.22, bf16[2560,1536]{1,0:T(8,128)(2,1)} %all-gather.5.cloned.1.call-done), kind=kOutput, calls=%fused_computation.29 | convolution fusion | flops 1518796800 | bytes 10420228 | tf_op jit(solution)/shard_map/dot_general | solution.py:223
  176.8 7.7 %fusion.11 = bf16[2560,384]{1,0:T(8,128)(2,1)} fusion(f32[2560,384]{1,0:T(8,128)S(1)} %get-tuple-element.64, bf16[2560,1536]{1,0:T(8,128)(2,1)} %all-gather.5.cloned.1.call-done, bf16[1,3072,768]{2,1,0:T(8,128)(2,1)} %param.20, s32[]{:T(128)S(6)} %select_n.22), kind=kOutput, calls=%fused_computation.15 | convolution fusion | flops 1528627200 | bytes 10420228 | tf_op jit(solution)/shard_map/dot_general | solution.py:45
  184.5 2.0 fusion.63
  186.6 53.0 %reduce-scatter.10.cloned.1.call-done = bf16[96,3072]{1,0:T(8,128)(2,1)} async-done(((bf16[768,3072]{1,0:T(8,128)(2,1)}), bf16[96,3072]{1,0:T(8,128)(2,1)}) %reduce-scatter.10.cloned.1.call-update) | async-done | bytes 589840
  239.6 0.9 slice.68
  240.5 0.2 copy.29
  240.7 0.1 copy.25
  240.8 1.0 slice.67
  241.9 0.3 copy.28
  242.2 0.3 copy.24
  242.5 1.0 maximum_bitcast_fusion
  243.5 1.0 fusion.77
  244.5 40.5 %all-reduce.1 = (f32[768]{0:T(1024)}, f32[32,12]{0,1:T(8,128)}, f32[768]{0:T(1024)}, f32[768,4]{0,1:T(4,128)}) all-reduce(f32[768]{0:T(1024)S(1)} %get-tuple-element.42, f32[32,12]{0,1:T(8,128)S(1)} %fusion.87, f32[768]{0:T(1024)S(1)} %copy-done.30, ...), channel_id=1, replica_groups=mesh['dp'=2,'context'=4,'expert'=4] {'dp','context','expert'}, use_global_device_ids=true, to_apply=%region_11.12 | all-reduce | flops 4992 | bytes 39936 | tf_op jit(solution)/shard_map/psum | solution.py:383
  285.0 5.6 %fusion.38 = f32[1,384,768]{2,1,0:T(8,128)} fusion(bf16[2560,384]{1,0:T(8,128)(2,1)} %get-tuple-element.39, bf16[2560,1536]{1,0:T(8,128)(2,1)} %all-gather.5.cloned.1.call-done), kind=kOutput, calls=%fused_computation.56 | convolution fusion | flops 1509949440 | bytes 7077888 | tf_op jit(solution)/shard_map/dot_general | solution.py:45
  290.6 5.4 %fusion.35 = f32[1,768,384]{2,1,0:T(8,128)} fusion(bf16[2560,384]{1,0:T(8,128)(2,1)S(1)} %copy-done.43, bf16[2560,1536]{1,0:T(8,128)(2,1)} %all-gather.5.cloned.1.call-done), kind=kOutput, calls=%fused_computation.55 | convolution fusion | flops 1509949440 | bytes 7077888 | tf_op jit(solution)/shard_map/dot_general | solution.py:45
  296.0 0.9 bitcast_convert_fusion
  296.9 0.7 slice.69
  297.6 0.7 slice.70
  (112 shorter events, 0.7 us)
Async XLA Ops:
  7.2 41.3 %copy-start = (bf16[768,768]{1,0:T(8,128)(2,1)S(1)}, bf16[768,768]{1,0:T(8,128)(2,1)}, u32[]{:S(2)}) copy-start(bf16[768,768]{1,0:T(8,128)(2,1)} %param.15) | copy-start | bytes 3538948
  7.2 26.3 %all-gather.3.cloned.1.call-start = ((), (), s32[]{:S(2)}) async-start(), calls=%async_computation.5 | async-start | bytes 1966080 | tf_op jit(solution)/shard_map/all_gather | solution.py:257
  9.1 2.0 copy-start.31
  11.0 120.9 %all-gather.5.cloned.1.call-start = ((), (), s32[]{:S(2)}) async-start(), calls=%async_computation.6 | async-start | bytes 8847360 | tf_op jit(solution)/shard_map/all_gather | solution.py:300
  38.2 10.8 %copy-start.2 = (bf16[1024,1536]{1,0:T(8,128)(2,1)}, bf16[1024,1536]{1,0:T(8,128)(2,1)S(1)}, u32[]{:S(2)}) copy-start(bf16[1024,1536]{1,0:T(8,128)(2,1)S(1)} %convolution_convert_fusion.k_ref.v_ref) | copy-start | bytes 9437188
  38.3 10.3 %copy-start.14 = (bf16[1,256,768]{2,1,0:T(8,128)(2,1)S(1)}, bf16[1,256,768]{2,1,0:T(8,128)(2,1)}, u32[]{:S(2)}) copy-start(bf16[1,256,768]{2,1,0:T(8,128)(2,1)} %param.12) | copy-start | bytes 1179652
  38.3 11.8 %copy-start.18 = (f32[768]{0:T(1024)S(1)}, f32[768]{0:T(1024)}, u32[]{:S(2)}) copy-start(f32[768]{0:T(1024)} %param.17) | copy-start | bytes 9220
  38.3 11.8 %copy-start.19 = (f32[768,4]{0,1:T(4,128)S(1)}, f32[768,4]{0,1:T(4,128)}, u32[]{:S(2)}) copy-start(f32[768,4]{0,1:T(4,128)} %param.18) | copy-start | bytes 36868
  38.3 12.7 %copy-start.24 = (s32[1,256]{1,0:T(1,128)S(1)}, s32[1,256]{1,0:T(1,128)}, u32[]{:S(2)}) copy-start(s32[1,256]{1,0:T(1,128)} %param.21) | copy-start | bytes 3076
  38.3 12.7 %copy-start.17 = (bf16[1,256,768]{2,1,0:T(8,128)(2,1)S(1)}, bf16[1,256,768]{2,1,0:T(8,128)(2,1)}, u32[]{:S(2)}) copy-start(bf16[1,256,768]{2,1,0:T(8,128)(2,1)} %param.23) | copy-start | bytes 1179652
  48.5 32.9 %copy-start.4 = (bf16[12,1024,256]{2,1,0:T(8,128)(2,1)}, bf16[12,1024,256]{2,1,0:T(8,128)(2,1)S(1)}, u32[]{:S(2)}) copy-start(bf16[12,1024,256]{2,1,0:T(8,128)(2,1)S(1)} %get-tuple-element.27.probs_ref) | copy-start | bytes 18874372
  48.5 3.1 %copy-start.39 = (s32[256]{0:T(256)S(1)}, s32[256]{0:T(256)}, u32[]{:S(2)}) copy-start(s32[256]{0:T(256)} %compare_select_fusion.1) | copy-start | bytes 3076
  49.1 78.8 %copy-start.10 = (f32[256,768]{1,0:T(8,128)}, f32[256,768]{1,0:T(8,128)S(1)}, u32[]{:S(2)}) copy-start(f32[256,768]{1,0:T(8,128)S(1)} %get-tuple-element.57) | copy-start | bytes 2359300
  50.1 1.1 copy-start.21
  51.0 0.6 copy-start.35
  81.4 103.1 %reduce-scatter.6.cloned.1.call-start = ((), (), s32[]{:S(2)}) async-start(), calls=%async_computation.7 | async-start | bytes 1966080 | tf_op jit(solution)/shard_map/reduce_scatter | solution.py:352
  81.9 5.1 %copy-start.15 = (bf16[4,80,1536]{2,1,0:T(8,128)(2,1)S(1)}, bf16[4,80,1536]{2,1,0:T(8,128)(2,1)}, u32[]{:S(2)}) copy-start(bf16[4,80,1536]{2,1,0:T(8,128)(2,1)} %all_to_all.10) | copy-start | bytes 2949124
  81.9 12.1 %slice-start = ((s8[4718592]{0:T(1024)(128)(4,1)}), s8[4194304]{0:T(1024)(128)(4,1)S(1)}, s32[]{:S(2)}) async-start(s8[4718592]{0:T(1024)(128)(4,1)} %bitcast.105), calls=%async_computation.10 | async-start | bytes 8388608
  82.0 13.9 %slice-start.2 = ((s8[4718592]{0:T(1024)(128)(4,1)}), s8[4194304]{0:T(1024)(128)(4,1)S(1)}, s32[]{:S(2)}) async-start(s8[4718592]{0:T(1024)(128)(4,1)} %bitcast.107), calls=%async_computation.12 | async-start | bytes 8388608
  87.1 7.0 %slice-start.1 = ((s8[4718592]{0:T(1024)(128)(4,1)}), s8[524288]{0:T(1024)(128)(4,1)S(1)}, s32[]{:S(2)}) async-start(s8[4718592]{0:T(1024)(128)(4,1)} %bitcast.105), calls=%async_computation.11 | async-start | bytes 1048576
  87.1 8.8 %slice-start.3 = ((s8[4718592]{0:T(1024)(128)(4,1)}), s8[524288]{0:T(1024)(128)(4,1)S(1)}, s32[]{:S(2)}) async-start(s8[4718592]{0:T(1024)(128)(4,1)} %bitcast.107), calls=%async_computation.13 | async-start | bytes 1048576
  97.6 27.1 %copy-start.40 = (s32[256]{0:T(256)S(1)}, s32[256]{0:T(256)}, u32[]{:S(2)}) copy-start(s32[256]{0:T(256)} %compare_select_fusion.1) | copy-start | bytes 3076
  97.6 27.7 %copy-start.36 = (f32[256]{0:T(256)S(1)}, f32[256]{0:T(256)}, u32[]{:S(2)}) copy-start(f32[256]{0:T(256)} %copy-done.35) | copy-start | bytes 3076
  97.7 28.6 %copy-start.25 = (s32[1,256]{1,0:T(1,128)S(1)}, s32[1,256]{1,0:T(1,128)}, u32[]{:S(2)}) copy-start(s32[1,256]{1,0:T(1,128)} %param.21) | copy-start | bytes 3076
  97.7 28.6 %copy-start.20 = (f32[768,4]{0,1:T(4,128)S(1)}, f32[768,4]{0,1:T(4,128)}, u32[]{:S(2)}) copy-start(f32[768,4]{0,1:T(4,128)} %param.18) | copy-start | bytes 36868
  97.7 28.6 %copy-start.22 = (f32[256]{0:T(256)S(1)}, f32[256]{0:T(256)}, u32[]{:S(2)}) copy-start(f32[256]{0:T(256)} %copy-done.21) | copy-start | bytes 3076
  124.7 3.3 %copy-start.38 = (f32[256]{0:T(256)S(1)}, f32[256]{0:T(256)}, u32[]{:S(2)}) copy-start(f32[256]{0:T(256)} %get-tuple-element.54) | copy-start | bytes 3076
  126.2 1.9 copy-start.28
  126.3 1.9 copy-start.33
  128.2 0.9 copy-start.12
  131.8 1.9 copy-start.3
  133.7 2.8 copy-start.5
  136.5 12.8 %copy-start.41 = (bf16[768,2304]{1,0:T(8,128)(2,1)S(1)}, bf16[768,2304]{1,0:T(8,128)(2,1)}, u32[]{:S(2)}) copy-start(bf16[768,2304]{1,0:T(8,128)(2,1)} %param.14) | copy-start | bytes 10616836
  149.3 1.5 copy-start.8
  149.3 1.7 copy-start.6
  153.6 1.9 copy-start.16
  153.6 2.4 copy-start.7
  153.6 86.0 %reduce-scatter.10.cloned.1.call-start = ((), (), s32[]{:S(2)}) async-start(), calls=%async_computation.9 | async-start | bytes 5308416
  153.7 2.4 copy-start.42
  156.0 1.5 copy-start.9
  168.2 1.1 copy-start.11
  168.2 1.1 copy-start.23
  168.2 1.1 copy-start.26
  168.2 1.1 copy-start.29
  168.2 1.1 copy-start.34
  168.3 127.7 %reduce-scatter.8.cloned.1.call-start = ((), (), s32[]{:S(2)}) async-start(), calls=%async_computation.8 | async-start | bytes 737280 | tf_op jit(solution)/shard_map/reduce_scatter | solution.py:380
  176.8 7.7 %copy-start.27 = (f32[768]{0:T(1024)S(1)}, f32[768]{0:T(1024)}, u32[]{:S(2)}) copy-start(f32[768]{0:T(1024)} %param.13) | copy-start | bytes 9220
  176.8 7.7 %copy-start.32 = (f32[256]{0:T(256)S(1)}, f32[256]{0:T(256)}, u32[]{:S(2)}) copy-start(f32[256]{0:T(256)} %copy-done.31) | copy-start | bytes 3076
  186.5 57.0 %copy-start.13 = (f32[256,768]{1,0:T(8,128)S(1)}, f32[256,768]{1,0:T(8,128)}, u32[]{:S(2)}) copy-start(f32[256,768]{1,0:T(8,128)} %copy-done.12) | copy-start | bytes 2359300
  186.5 57.0 %copy-start.37 = (f32[256]{0:T(256)S(1)}, f32[256]{0:T(256)}, u32[]{:S(2)}) copy-start(f32[256]{0:T(256)} %get-tuple-element.52) | copy-start | bytes 3076
  240.5 4.0 %copy-start.30 = (f32[768]{0:T(1024)S(1)}, f32[768]{0:T(1024)}, u32[]{:S(2)}) copy-start(f32[768]{0:T(1024)} %get-tuple-element.40) | copy-start | bytes 9220
  285.0 5.6 %copy-start.43 = (bf16[2560,384]{1,0:T(8,128)(2,1)S(1)}, bf16[2560,384]{1,0:T(8,128)(2,1)}, u32[]{:S(2)}) copy-start(bf16[2560,384]{1,0:T(8,128)(2,1)} %fusion.11) | copy-start | bytes 5898244
  285.0 13.3 %copy-start.1 = (bf16[768,768]{1,0:T(8,128)(2,1)S(1)}, bf16[768,768]{1,0:T(8,128)(2,1)}, u32[]{:S(2)}) copy-start(bf16[768,768]{1,0:T(8,128)(2,1)} %param.15) | copy-start | bytes 3538948
Sparse Core Ops, SparseCore 0:
  11.1 22.3 all-gather.2
  81.5 50.3 all-gather.4
  153.7 28.1 reduce-scatter.5
  185.6 53.9 reduce-scatter.9
  243.6 21.9 reduce-scatter.7
